TPU v7x, 128 devices: a whole 4x4x4 slice. The times are simulated.
128 devices in a mesh: rows: 32 (over z, x_hi, y), feat: 4 (over x_lo, core).
Axes of the slice: x: 4 (x_hi: 2, x_lo: 2; x = x_hi * 2 + x_lo), y: 4, z: 4, core: 2. Of those that a mesh axis runs over, the one named last changes fastest.
Arguments:
- slab: float32 [16384, 2048], P('rows', 'feat'), may hold values from -42 to 42
- cov_old: float32 [2048, 2048], P('rows', 'feat'), may hold values from -4.5 to 4.5, as said below
Outputs:
- whitened: float32 [16384, 2048], P('rows', 'feat')
- factor: float32 [2048, 2048], P('rows', 'feat')
Inputs may be any that keep to these rules, and one draw needn't show every extreme that they name: `cov_old`: symmetric.
All inputs are finite; a program needn't handle non-finite values.
Results may differ from a plain program's by a relative error of at most 0.000098.
Values sent between devices are 32-bit elements; how exact they have to be, the bound alone decides.
A program may use at most 192 MiB of HBM per device.

v0:
```python
import jax
import jax.numpy as jnp
from jax import lax
from jax.sharding import PartitionSpec as P


def broadcast(shard, axis, root):
    mine = lax.axis_index(axis) == root
    return lax.psum(jnp.where(mine, shard, jnp.zeros_like(shard)), axis)


def matmul(left, right):
    return jnp.dot(left, right, precision=lax.Precision.HIGHEST, preferred_element_type=jnp.float32)


def invert_diag(diag_factor):
    identity = jnp.eye(diag_factor.shape[0], dtype=jnp.float32)
    return lax.linalg.triangular_solve(diag_factor, identity, left_side=True, lower=True)


def invert_lower(factor_full, width, n_feat):
    diag_inverses = []
    for block in range(n_feat):
        low = block * width
        diag_inverses.append(invert_diag(factor_full[low : low + width, low : low + width]))
    dim = width * n_feat
    inverse = jnp.zeros((dim, dim), jnp.float32)
    for col in range(n_feat):
        cl = col * width
        known = diag_inverses[col]
        inverse = inverse.at[cl : cl + width, cl : cl + width].set(known)
        for row in range(col + 1, n_feat):
            rl = row * width
            partial_sum = matmul(
                factor_full[rl : rl + width, cl:rl], inverse[cl:rl, cl : cl + width]
            )
            inverse = inverse.at[rl : rl + width, cl : cl + width].set(
                -matmul(diag_inverses[row], partial_sum)
            )
    return inverse


def per_device(slab, cov_old):
    n_rows = lax.axis_size("rows")
    n_feat = lax.axis_size("feat")
    row_index = lax.axis_index("rows")
    feat_index = lax.axis_index("feat")
    rows_dev, width = slab.shape
    dim = width * n_feat
    total = rows_dev * n_rows
    cov_rows = cov_old.shape[0]
    column_sums = lax.psum(jnp.sum(slab, axis=0), "rows")
    centered = slab - (column_sums / total)[None, :]
    full_rows = lax.all_gather(centered, "feat", axis=1, tiled=True)
    contract = (((0,), (0,)), ((), ()))
    own_rows = lax.psum_scatter(
        lax.dot_general(
            full_rows,
            centered,
            contract,
            precision=lax.Precision.HIGHEST,
            preferred_element_type=jnp.float32,
        )
        / total,
        "rows",
        scatter_dimension=0,
        tiled=True,
    )
    column = lax.all_gather(cov_old + own_rows, "rows", axis=0, tiled=True)
    factor_full = jnp.zeros((dim, dim), jnp.float32)
    identity = jnp.eye(width, dtype=jnp.float32)
    for step in range(n_feat):
        lower_part = column[step * width :]
        is_root = feat_index == step
        diag_block = jnp.where(is_root, lower_part[:width], identity)
        below = jnp.where(is_root, lower_part, 0.0)
        diag_factor = jnp.tril(lax.linalg.cholesky(diag_block))
        diag_inverse = invert_diag(diag_factor)
        panel_local = lax.dot_general(
            below,
            diag_inverse,
            (((1,), (1,)), ((), ())),
            precision=lax.Precision.HIGHEST,
            preferred_element_type=jnp.float32,
        )
        panel_all = broadcast(panel_local, "feat", step)
        factor_full = factor_full.at[step * width :, step * width : (step + 1) * width].set(
            panel_all
        )
        if step + 1 < n_feat:
            span = panel_all.shape[0]
            start = jnp.clip((feat_index - step) * width, 0, span - width)
            partner = lax.dynamic_slice_in_dim(panel_all, start, width, 0)
            update = lax.dot_general(
                panel_all,
                partner,
                (((1,), (1,)), ((), ())),
                precision=lax.Precision.HIGHEST,
                preferred_element_type=jnp.float32,
            )
            update = jnp.where(feat_index > step, update, 0.0)
            column = column.at[step * width :].add(-update)
    inverse = invert_lower(factor_full, width, n_feat)
    quarter = rows_dev // n_feat
    my_rows = lax.dynamic_slice_in_dim(full_rows, feat_index * quarter, quarter, 0)
    solved = lax.dot_general(
        my_rows,
        inverse,
        (((1,), (1,)), ((), ())),
        precision=lax.Precision.HIGHEST,
        preferred_element_type=jnp.float32,
    )
    whitened = lax.all_to_all(solved, "feat", split_axis=1, concat_axis=0, tiled=True)
    factor_rows = lax.dynamic_slice_in_dim(factor_full, row_index * cov_rows, cov_rows, 0)
    factor_out = lax.dynamic_slice_in_dim(factor_rows, feat_index * width, width, 1)
    return (whitened, factor_out)


def solution(mesh):
    placed = (P("rows", "feat"), P("rows", "feat"))
    return jax.shard_map(
        per_device,
        mesh=mesh,
        in_specs=placed,
        out_specs=(P("rows", "feat"), P("rows", "feat")),
        check_vma=False,
    )
```

profile of v0, /device:TPU:1, one launch (start us, length us, event | category | flops | bytes accessed | tf_op | source)
XLA Modules:
  0.0 1699.8 jit_solution(12982457571958026488)
XLA Ops:
  8.5 84.5 %psum.35 = f32[512]{0:T(512)S(1)} all-reduce(f32[512]{0:T(512)S(1)} %reduce_sum.9), channel_id=1, replica_groups=mesh['rows'=32,'feat'=4] {'rows'}, use_global_device_ids=true, to_apply=%region_1.0 | all-reduce | flops 512 | bytes 4096 | tf_op jit(solution)/shard_map/psum | solution.py:52
  95.5 55.0 %all-gather.3.cloned.1.call-done = f32[512,2048]{1,0:T(8,128)} async-done(((f32[512,512]{1,0:T(8,128)}), f32[512,2048]{1,0:T(8,128)}) %all-gather.3.cloned.1.call-update) | async-done | bytes 4194320 | tf_op jit(solution)/shard_map/all_gather | solution.py:54
  160.7 169.8 %reduce-scatter.4.cloned.1.call-done = f32[64,512]{1,0:T(8,128)} async-done(((f32[2048,512]{1,0:T(8,128)}), f32[64,512]{1,0:T(8,128)}) %reduce-scatter.4.cloned.1.call-update) | async-done | bytes 131088 | tf_op jit(solution)/shard_map/reduce_scatter | solution.py:56
  332.2 99.9 %all-gather.5.cloned.1.call-done = f32[2048,512]{1,0:T(8,128)} async-done(((f32[64,512]{1,0:T(8,128)}), f32[2048,512]{1,0:T(8,128)}) %all-gather.5.cloned.1.call-update) | async-done | bytes 4194320 | tf_op jit(solution)/shard_map/all_gather | solution.py:69
  442.0 11.7 custom-call.55
  466.5 11.7 custom-call.57
  490.3 11.7 custom-call.59
  513.7 11.9 custom-call.61
  538.9 39.3 %custom-call.62 = f32[4,128,128]{1,2,0:T(8,128)S(1)} custom-call(f32[4,128,128]{2,1,0:T(8,128)S(1)} %get-tuple-element.266), custom_call_target="InvertDiagBlocksLowerTriangular" | custom-call | tf_op jit(solution)/shard_map/triangular_solve/custom-call.3 | solution.py:18
  591.7 91.2 %all-reduce.8.cloned.1.call-done = f32[2048,512]{0,1:T(8,128)} async-done(((f32[2048,512]{0,1:T(8,128)}), f32[2048,512]{0,1:T(8,128)}) %all-reduce.8.cloned.1.call-update) | async-done | bytes 4194320 | tf_op jit(solution)/shard_map/psum | solution.py:9
  698.4 11.7 custom-call.63
  722.9 11.7 custom-call.65
  746.4 11.7 custom-call.67
  769.9 12.1 custom-call.69
  795.4 39.3 %custom-call.70 = f32[4,128,128]{1,2,0:T(8,128)S(1)} custom-call(f32[4,128,128]{2,1,0:T(8,128)S(1)} %get-tuple-element.267), custom_call_target="InvertDiagBlocksLowerTriangular" | custom-call | tf_op jit(solution)/shard_map/triangular_solve/custom-call.3 | solution.py:18
  846.7 75.4 %all-reduce.10.cloned.1.call-done = f32[1536,512]{0,1:T(8,128)} async-done(((f32[1536,512]{0,1:T(8,128)}), f32[1536,512]{0,1:T(8,128)}) %all-reduce.10.cloned.1.call-update) | async-done | bytes 3145744 | tf_op jit(solution)/shard_map/psum | solution.py:9
  1007.5 11.9 custom-call.77
  1033.8 39.3 %custom-call.78 = f32[4,128,128]{1,2,0:T(8,128)S(1)} custom-call(f32[4,128,128]{2,1,0:T(8,128)S(1)} %get-tuple-element.268), custom_call_target="InvertDiagBlocksLowerTriangular" | custom-call | tf_op jit(solution)/shard_map/triangular_solve/custom-call.3 | solution.py:18
  1086.9 54.4 %all-reduce.12.cloned.1.call-done = f32[1024,512]{0,1:T(8,128)} async-done(((f32[1024,512]{0,1:T(8,128)}), f32[1024,512]{0,1:T(8,128)}) %all-reduce.12.cloned.1.call-update) | async-done | bytes 2097168 | tf_op jit(solution)/shard_map/psum | solution.py:9
  1174.6 12.1 custom-call.81
  1197.6 11.7 custom-call.83
  1238.5 12.3 while.37
  1251.6 40.3 %custom-call.86 = f32[4,128,128]{1,2,0:T(8,128)S(1)} custom-call(f32[4,128,128]{2,1,0:T(8,128)} %copy-done.22), custom_call_target="InvertDiagBlocksLowerTriangular" | custom-call | tf_op jit(solution)/shard_map/triangular_solve/custom-call.3 | solution.py:18
  1317.7 27.6 %all-reduce.14.cloned.1.call-done = f32[512,512]{0,1:T(8,128)} async-done(((f32[512,512]{0,1:T(8,128)}), f32[512,512]{0,1:T(8,128)}) %all-reduce.14.cloned.1.call-update) | async-done | bytes 1048592 | tf_op jit(solution)/shard_map/psum | solution.py:9
  1363.3 39.7 %custom-call.87 = f32[4,128,128]{1,2,0:T(8,128)S(1)} custom-call(f32[4,128,128]{2,1,0:T(8,128)S(1)} %get-tuple-element.270), custom_call_target="InvertDiagBlocksLowerTriangular" | custom-call | tf_op jit(solution)/shard_map/triangular_solve/custom-call.3 | solution.py:18
  1424.2 39.5 %custom-call.88 = f32[4,128,128]{1,2,0:T(8,128)S(1)} custom-call(f32[4,128,128]{2,1,0:T(8,128)S(1)} %get-tuple-element.271), custom_call_target="InvertDiagBlocksLowerTriangular" | custom-call | tf_op jit(solution)/shard_map/triangular_solve/custom-call.3 | solution.py:18
  1490.8 12.5 while.40
  1503.3 39.3 %custom-call.89 = f32[4,128,128]{1,2,0:T(8,128)S(1)} custom-call(f32[4,128,128]{2,1,0:T(8,128)S(1)} %get-tuple-element.272), custom_call_target="InvertDiagBlocksLowerTriangular" | custom-call | tf_op jit(solution)/shard_map/triangular_solve/custom-call.3 | solution.py:18
  1557.1 13.8 fusion.7
  1570.9 11.9 while.41
  1583.5 40.3 %custom-call.90 = f32[4,128,128]{1,2,0:T(8,128)S(1)} custom-call(f32[4,128,128]{2,1,0:T(8,128)} %copy-done.21), custom_call_target="InvertDiagBlocksLowerTriangular" | custom-call | tf_op jit(solution)/shard_map/triangular_solve/custom-call.3 | solution.py:18
  1652.2 21.0 %fusion.79 = f32[128,2048]{1,0:T(8,128)S(1)} fusion(f32[2048,2048]{1,0:T(8,128)} %constant_dynamic-update-slice_fusion.18, f32[512,2048]{1,0:T(8,128)} %all-gather.3.cloned.1.call-done, s32[]{:T(128)S(6)} %select_n.137), kind=kOutput, calls=%fused_computation.171 | convolution fusion | flops 6442450944 | bytes 18874372 | tf_op jit(solution)/shard_map/dot_general | solution.py:106
  (479 shorter events, 578.3 us)
Async XLA Ops:
  7.2 143.3 %all-gather.3.cloned.1.call-start = ((), (), s32[]{:S(2)}) async-start(), calls=%async_computation.2 | async-start | bytes 5242880 | tf_op jit(solution)/shard_map/all_gather | solution.py:54
  95.4 235.1 %reduce-scatter.4.cloned.1.call-start = ((), (), s32[]{:S(2)}) async-start(), calls=%async_computation.8 | async-start | bytes 4325376 | tf_op jit(solution)/shard_map/reduce_scatter | solution.py:56
  160.6 169.9 %copy-start.23 = (f32[64,512]{1,0:T(8,128)S(1)}, f32[64,512]{1,0:T(8,128)}, u32[]{:S(2)}) copy-start(f32[64,512]{1,0:T(8,128)} %param.42) | copy-start | bytes 393220
  160.6 271.6 %all-gather.5.cloned.1.call-start = ((), (), s32[]{:S(2)}) async-start(), calls=%async_computation.3 | async-start | bytes 4325376 | tf_op jit(solution)/shard_map/all_gather | solution.py:69
  332.1 350.8 %all-reduce.8.cloned.1.call-start = ((), (), s32[]{:S(2)}) async-start(), calls=%async_computation.4 | async-start | bytes 8388608 | tf_op jit(solution)/shard_map/psum | solution.py:9
  440.9 1.0 copy-start.18
  578.2 4.8 copy-start.1
  591.7 330.4 %all-reduce.10.cloned.1.call-start = ((), (), s32[]{:S(2)}) async-start(), calls=%async_computation.5 | async-start | bytes 6291456 | tf_op jit(solution)/shard_map/psum | solution.py:9
  693.4 2.0 copy-start.2
  697.3 1.0 copy-start.19
  834.7 4.8 copy-start.3
  846.6 294.7 %all-reduce.12.cloned.1.call-start = ((), (), s32[]{:S(2)}) async-start(), calls=%async_computation.6 | async-start | bytes 4194304 | tf_op jit(solution)/shard_map/psum | solution.py:9
  931.1 1.7 copy-start.4
  934.7 1.0 copy-start.20
  1073.1 4.8 copy-start.5
  1082.9 262.5 %all-reduce.14.cloned.1.call-start = ((), (), s32[]{:S(2)}) async-start(), calls=%async_computation.7 | async-start | bytes 2097152 | tf_op jit(solution)/shard_map/psum | solution.py:9
  1141.3 7.2 copy-start.8
  1147.1 1.3 copy-start.10
  1238.5 61.1 %copy-start.9 = (f32[1024,512]{0,1:T(8,128)S(1)}, f32[1024,512]{0,1:T(8,128)}, u32[]{:S(2)}) copy-start(f32[1024,512]{0,1:T(8,128)} %slice.852) | copy-start | bytes 6291460
  1250.9 0.7 copy-start.22
  1291.9 7.7 copy-start.11
  1305.8 7.9 copy-start.6
  1313.6 2.6 copy-start.7
  1424.2 41.0 %copy-start.17 = (f32[512,512]{0,1:T(8,128)}, f32[512,512]{0,1:T(8,128)S(1)}, u32[]{:S(2)}) copy-start(f32[512,512]{0,1:T(8,128)S(1)} %get-tuple-element.878) | copy-start | bytes 3145732
  1473.4 3.4 copy-start.14
  1478.7 5.7 copy-start
  1543.1 11.1 copy-start.16
  1582.8 0.7 copy-start.21
  1623.8 7.5 copy-start.15
  1628.1 7.3 copy-start.12
  1638.3 10.0 copy-start.13
  1674.3 17.4 %all-to-all-start = ((f32[128,4,512]{2,0,1:T(8,128)}), f32[128,4,512]{2,0,1:T(8,128)S(1)}, u32[]{:S(2)}, u32[]{:S(2)}) async-start(f32[128,4,512]{2,0,1:T(8,128)} %bitcast.273), calls=%async_computation | async-start | bytes 2097152 | tf_op jit(solution)/shard_map/all_to_all | solution.py:113
Sparse Core Ops, SparseCore 0:
  95.5 54.9 all-gather.2
  160.7 169.6 reduce-scatter.3
  334.1 98.0 all-gather.4
  591.8 91.0 all-reduce.7
  846.7 75.3 all-reduce.9
  1083.0 58.2 all-reduce.11
  1302.8 42.4 all-reduce.13
where the time goes:
time: 1710 us; the launch traced here: 1700 us
  other arithmetic  664 us (39%)
  waiting for transfers between devices  585 us (34%)
  matrix products  205 us (12%)
  local copies, waits for them, and re-layouts  130 us (8%)
  blocking collectives  84.5 us (5%)
  between operations  26.2 us (2%)
    another operation x16, other arithmetic, invert_diag(): lax.linalg.triangular_solve(diag_factor, identity, left_side=True, lower=...  326 us
    another operation x59, other arithmetic, per_device(): diag_factor = jnp.tril(lax.linalg.cholesky(diag_block))  318 us
    psum x4, waiting for transfers between devices, broadcast(): return lax.psum(jnp.where(mine, shard, jnp.zeros_like(shard)), axis)  249 us
    reduce_scatter x1, waiting for transfers between devices, per_device(): lax.psum_scatter(lax.dot_general(full_rows, centered, contract, precision...  170 us
    all_gather x1, waiting for transfers between devices, per_device(): column = lax.all_gather(cov_old + own_rows, 'rows', axis=0, tiled=True)  99.9 us
    psum x1, blocking collectives, per_device(): column_sums = lax.psum(jnp.sum(slab, axis=0), 'rows')  84.5 us
    another operation x169, local copies, waits for them, and re-layouts, invert_diag(): lax.linalg.triangular_solve(diag_factor, identity, left_side=True, lower=...  81.2 us
    all_gather x1, waiting for transfers between devices, per_device(): full_rows = lax.all_gather(centered, 'feat', axis=1, tiled=True)  55 us
  transfers between devices with their start and end apart: 8, of which 8 were waited for; matrix products, arithmetic and copies ran while one was open for 1% of the time, Pallas kernels for 0%

commit v1 on v0

--- a/solution.py
+++ b/solution.py
@@ -6,7 +6,7 @@
 
 def broadcast(shard, axis, root):
     mine = lax.axis_index(axis) == root
-    return lax.psum(jnp.where(mine, shard, jnp.zeros_like(shard)), axis)
+    return jnp.sum(lax.all_gather(jnp.where(mine, shard, jnp.zeros_like(shard)), axis), axis=0)
 
 
 def matmul(left, right):

time: 1710 us -> 1950 us (1.14)
  waiting for transfers between devices: 585 us -> 715 us
  local copies, waits for them, and re-layouts: 130 us -> 190 us
  other arithmetic: 664 us -> 708 us
    all_gather x0 -> x4, waiting for transfers between devices: none -> 379 us  [broadcast(): lax.all_gather(jnp.where(mine, shard, jnp.zeros_like(shard)), axis)]
    psum x4 -> x0, waiting for transfers between devices: 249 us -> none  [broadcast(): return lax.psum(jnp.where(mine, shard, jnp.zeros_like(shard)), axis)]
    all_gather x0 -> x4, local copies, waits for them, and re-layouts: none -> 53.2 us  [broadcast(): lax.all_gather(jnp.where(mine, shard, jnp.zeros_like(shard)), axis)]
    reduce_sum x0 -> x4, other arithmetic: none -> 40.9 us  [broadcast(): jnp.sum(lax.all_gather(jnp.where(mine, shard, jnp.zeros_like(shard)), axi...]
where the time goes in v1:
time: 1950 us; the launch traced here: 1940 us
  waiting for transfers between devices  715 us (37%)
  other arithmetic  708 us (36%)
  matrix products  209 us (11%)
  local copies, waits for them, and re-layouts  190 us (10%)
  blocking collectives  84.5 us (4%)
  between operations  26.2 us (1%)
    all_gather x4, waiting for transfers between devices, broadcast(): lax.all_gather(jnp.where(mine, shard, jnp.zeros_like(shard)), axis)  379 us
    another operation x16, other arithmetic, invert_diag(): lax.linalg.triangular_solve(diag_factor, identity, left_side=True, lower=...  326 us
    another operation x59, other arithmetic, per_device(): diag_factor = jnp.tril(lax.linalg.cholesky(diag_block))  318 us
    reduce_scatter x1, waiting for transfers between devices, per_device(): lax.psum_scatter(lax.dot_general(full_rows, centered, contract, precision...  170 us
    all_gather x1, waiting for transfers between devices, per_device(): column = lax.all_gather(cov_old + own_rows, 'rows', axis=0, tiled=True)  99.9 us
    psum x1, blocking collectives, per_device(): column_sums = lax.psum(jnp.sum(slab, axis=0), 'rows')  84.5 us
    another operation x169, local copies, waits for them, and re-layouts, invert_diag(): lax.linalg.triangular_solve(diag_factor, identity, left_side=True, lower=...  81 us
    all_gather x1, waiting for transfers between devices, per_device(): full_rows = lax.all_gather(centered, 'feat', axis=1, tiled=True)  55 us
  transfers between devices with their start and end apart: 8, of which 8 were waited for; matrix products, arithmetic and copies ran while one was open for 1% of the time, Pallas kernels for 0%

profile of v1, /device:TPU:1, one launch (start us, length us, event | category | flops | bytes accessed | tf_op | source)
XLA Modules:
  0.0 1937.9 jit_solution(13478760472927297198)
XLA Ops:
  8.5 84.5 %psum.7 = f32[512]{0:T(512)S(1)} all-reduce(f32[512]{0:T(512)S(1)} %reduce_sum.45), channel_id=1, replica_groups=mesh['rows'=32,'feat'=4] {'rows'}, use_global_device_ids=true, to_apply=%region_1.0 | all-reduce | flops 512 | bytes 4096 | tf_op jit(solution)/shard_map/psum | solution.py:52
  95.5 55.0 %all-gather.11.cloned.1.call-done = f32[512,2048]{1,0:T(8,128)} async-done(((f32[512,512]{1,0:T(8,128)}), f32[512,2048]{1,0:T(8,128)}) %all-gather.11.cloned.1.call-update) | async-done | bytes 4194320 | tf_op jit(solution)/shard_map/all_gather | solution.py:54
  160.7 169.7 %reduce-scatter.4.cloned.1.call-done = f32[64,512]{1,0:T(8,128)} async-done(((f32[2048,512]{1,0:T(8,128)}), f32[64,512]{1,0:T(8,128)}) %reduce-scatter.4.cloned.1.call-update) | async-done | bytes 131088 | tf_op jit(solution)/shard_map/reduce_scatter | solution.py:56
  332.2 99.9 %all-gather.13.cloned.1.call-done = f32[2048,512]{1,0:T(8,128)} async-done(((f32[64,512]{1,0:T(8,128)}), f32[2048,512]{1,0:T(8,128)}) %all-gather.13.cloned.1.call-update) | async-done | bytes 4194320 | tf_op jit(solution)/shard_map/all_gather | solution.py:69
  442.1 11.7 custom-call.55
  490.2 11.7 custom-call.59
  513.6 12.1 custom-call.61
  538.9 39.3 %custom-call.62 = f32[4,128,128]{1,2,0:T(8,128)S(1)} custom-call(f32[4,128,128]{2,1,0:T(8,128)S(1)} %get-tuple-element.266), custom_call_target="InvertDiagBlocksLowerTriangular" | custom-call | tf_op jit(solution)/shard_map/triangular_solve/custom-call.3 | solution.py:18
  591.7 150.9 %all-gather.15.cloned.1.call-done = f32[8192,512]{0,1:T(8,128)} async-done(((f32[2048,512]{0,1:T(8,128)}), f32[8192,512]{0,1:T(8,128)}) %all-gather.15.cloned.1.call-update) | async-done | bytes 16777232 | tf_op jit(solution)/shard_map/all_gather | solution.py:9
  742.6 20.4 %reshape.605 = f32[4,2048,512]{1,0,2:T(4,128)} reshape(f32[8192,512]{0,1:T(8,128)} %all-gather.15.cloned.1.call-done) | data formatting | bytes 33554432 | tf_op jit(solution)/shard_map/all_gather | solution.py:9
  763.1 15.0 reduce_sum.46
  865.1 11.9 custom-call.69
  891.4 39.3 %custom-call.70 = f32[4,128,128]{1,2,0:T(8,128)S(1)} custom-call(f32[4,128,128]{2,1,0:T(8,128)S(1)} %get-tuple-element.267), custom_call_target="InvertDiagBlocksLowerTriangular" | custom-call | tf_op jit(solution)/shard_map/triangular_solve/custom-call.3 | solution.py:18
  942.6 117.2 %all-gather.17.cloned.1.call-done = f32[6144,512]{0,1:T(8,128)} async-done(((f32[1536,512]{0,1:T(8,128)}), f32[6144,512]{0,1:T(8,128)}) %all-gather.17.cloned.1.call-update) | async-done | bytes 12582928 | tf_op jit(solution)/shard_map/all_gather | solution.py:9
  1059.8 15.4 reshape.606
  1075.2 12.6 reduce_sum.47
  1173.3 12.1 custom-call.77
  1199.8 39.3 %custom-call.78 = f32[4,128,128]{1,2,0:T(8,128)S(1)} custom-call(f32[4,128,128]{2,1,0:T(8,128)S(1)} %get-tuple-element.268), custom_call_target="InvertDiagBlocksLowerTriangular" | custom-call | tf_op jit(solution)/shard_map/triangular_solve/custom-call.3 | solution.py:18
  1252.3 79.2 %all-gather.19.cloned.1.call-done = f32[4096,512]{0,1:T(8,128)} async-done(((f32[1024,512]{0,1:T(8,128)}), f32[4096,512]{0,1:T(8,128)}) %all-gather.19.cloned.1.call-update) | async-done | bytes 8388624 | tf_op jit(solution)/shard_map/all_gather | solution.py:9
  1367.3 11.9 custom-call.79
  1418.7 12.1 custom-call.83
  1463.9 11.9 while.37
  1476.4 40.3 %custom-call.86 = f32[4,128,128]{1,2,0:T(8,128)S(1)} custom-call(f32[4,128,128]{2,1,0:T(8,128)} %copy-done.22), custom_call_target="InvertDiagBlocksLowerTriangular" | custom-call | tf_op jit(solution)/shard_map/triangular_solve/custom-call.3 | solution.py:18
  1543.3 31.7 %all-gather.21.cloned.1.call-done = f32[2048,512]{0,1:T(8,128)} async-done(((f32[512,512]{0,1:T(8,128)}), f32[2048,512]{0,1:T(8,128)}) %all-gather.21.cloned.1.call-update) | async-done | bytes 4194320 | tf_op jit(solution)/shard_map/all_gather | solution.py:9
  1602.9 39.3 %custom-call.87 = f32[4,128,128]{1,2,0:T(8,128)S(1)} custom-call(f32[4,128,128]{2,1,0:T(8,128)S(1)} %get-tuple-element.270), custom_call_target="InvertDiagBlocksLowerTriangular" | custom-call | tf_op jit(solution)/shard_map/triangular_solve/custom-call.3 | solution.py:18
  1663.4 39.5 %custom-call.88 = f32[4,128,128]{1,2,0:T(8,128)S(1)} custom-call(f32[4,128,128]{2,1,0:T(8,128)S(1)} %get-tuple-element.271), custom_call_target="InvertDiagBlocksLowerTriangular" | custom-call | tf_op jit(solution)/shard_map/triangular_solve/custom-call.3 | solution.py:18
  1730.0 12.0 while.40
  1742.0 39.3 %custom-call.89 = f32[4,128,128]{1,2,0:T(8,128)S(1)} custom-call(f32[4,128,128]{2,1,0:T(8,128)S(1)} %get-tuple-element.272), custom_call_target="InvertDiagBlocksLowerTriangular" | custom-call | tf_op jit(solution)/shard_map/triangular_solve/custom-call.3 | solution.py:18
  1795.8 13.8 fusion.7
  1809.6 12.0 while.41
  1822.3 40.3 %custom-call.90 = f32[4,128,128]{1,2,0:T(8,128)S(1)} custom-call(f32[4,128,128]{2,1,0:T(8,128)} %copy-done.21), custom_call_target="InvertDiagBlocksLowerTriangular" | custom-call | tf_op jit(solution)/shard_map/triangular_solve/custom-call.3 | solution.py:18
  1891.0 21.0 %fusion.79 = f32[128,2048]{1,0:T(8,128)S(1)} fusion(f32[2048,2048]{1,0:T(8,128)} %constant_dynamic-update-slice_fusion.18, f32[512,2048]{1,0:T(8,128)} %all-gather.11.cloned.1.call-done, s32[]{:T(128)S(6)} %select_n.137), kind=kOutput, calls=%fused_computation.171 | convolution fusion | flops 6442450944 | bytes 18874372 | tf_op jit(solution)/shard_map/dot_general | solution.py:106
  (487 shorter events, 670.2 us)
Async XLA Ops:
  7.2 143.3 %all-gather.11.cloned.1.call-start = ((), (), s32[]{:S(2)}) async-start(), calls=%async_computation.2 | async-start | bytes 5242880 | tf_op jit(solution)/shard_map/all_gather | solution.py:54
  95.4 235.0 %reduce-scatter.4.cloned.1.call-start = ((), (), s32[]{:S(2)}) async-start(), calls=%async_computation.8 | async-start | bytes 4325376 | tf_op jit(solution)/shard_map/reduce_scatter | solution.py:56
  160.6 169.8 %copy-start.23 = (f32[64,512]{1,0:T(8,128)S(1)}, f32[64,512]{1,0:T(8,128)}, u32[]{:S(2)}) copy-start(f32[64,512]{1,0:T(8,128)} %param.42) | copy-start | bytes 393220
  160.6 271.4 %all-gather.13.cloned.1.call-start = ((), (), s32[]{:S(2)}) async-start(), calls=%async_computation.3 | async-start | bytes 4325376 | tf_op jit(solution)/shard_map/all_gather | solution.py:69
  332.0 410.6 %all-gather.15.cloned.1.call-start = ((), (), s32[]{:S(2)}) async-start(), calls=%async_computation.4 | async-start | bytes 20971520 | tf_op jit(solution)/shard_map/all_gather | solution.py:9
  441.0 1.0 copy-start.17
  578.2 4.8 copy-start.1
  591.6 468.2 %all-gather.17.cloned.1.call-start = ((), (), s32[]{:S(2)}) async-start(), calls=%async_computation.5 | async-start | bytes 15728640 | tf_op jit(solution)/shard_map/all_gather | solution.py:9
  788.3 2.0 copy-start.2
  792.3 1.0 copy-start.18
  930.7 4.8 copy-start.3
  942.5 388.9 %all-gather.19.cloned.1.call-start = ((), (), s32[]{:S(2)}) async-start(), calls=%async_computation.6 | async-start | bytes 10485760 | tf_op jit(solution)/shard_map/all_gather | solution.py:9
  1097.1 1.8 copy-start.5
  1100.7 1.0 copy-start.19
  1239.1 4.8 copy-start.6
  1249.0 326.1 %all-gather.21.cloned.1.call-start = ((), (), s32[]{:S(2)}) async-start(), calls=%async_computation.7 | async-start | bytes 5242880 | tf_op jit(solution)/shard_map/all_gather | solution.py:9
  1350.9 5.1 copy-start.7
  1354.6 1.3 copy-start.9
  1366.3 1.0 copy-start.20
  1475.7 0.7 copy-start.22
  1516.7 7.8 copy-start.8
  1516.7 7.8 copy-start.10
  1531.3 8.7 copy-start.4
  1663.4 41.0 %copy-start.16 = (f32[512,512]{0,1:T(8,128)}, f32[512,512]{0,1:T(8,128)S(1)}, u32[]{:S(2)}) copy-start(f32[512,512]{0,1:T(8,128)S(1)} %get-tuple-element.879) | copy-start | bytes 3145732
  1712.6 3.4 copy-start.13
  1717.9 5.7 copy-start
  1781.8 11.1 copy-start.15
  1821.6 0.7 copy-start.21
  1862.6 7.5 copy-start.14
  1866.8 7.3 copy-start.11
  1877.1 10.0 copy-start.12
  1913.1 16.8 all-to-all-start
Sparse Core Ops, SparseCore 0:
  95.5 54.9 all-gather.10
  160.7 169.6 reduce-scatter.3
  334.0 97.9 all-gather.12
  591.7 150.8 all-gather.14
  942.7 117.1 all-gather.16
  1249.1 82.2 all-gather.18
  1527.6 47.3 all-gather.20
